TPU v7x, 32 devices: a whole 2x2x4 slice. The times are simulated.
32 devices in a mesh: parts: 2 (over x), sta: 16 (over z, y, core).
Axes of the slice: x: 2, y: 2, z: 4, core: 2. Of those that a mesh axis runs over, the one named last changes fastest.
Arguments:
- raw_traces: bfloat16 [512, 16384], P('parts', 'sta'), parts along dimension 0, may hold values from -6 to 6
- filter_taps: bfloat16 [256], replicated, may hold values from -0.375 to 0.375
- station_order: int32 [512], P('parts'), parts along dimension 0, may hold values from 0 to 255, each once
- window_starts: int32 [32], P('parts'), parts along dimension 0, may hold values from 0 to 2048, as said below
- pairing: int32 [4, 16], replicated, may hold values from 0 to 15, as said below
Outputs:
- correlation: float32 [4, 512, 16, 256], P(None, ('parts', 'sta')), parts along dimension 1
There are 2 independent parts, one for each index of `parts`. A program takes and returns all parts, laid end to end along the dimension named above; an argument that names none is the same for every part. Nothing has to cross between parts.
Inputs may be any that keep to these rules, and one draw needn't show every extreme that they name: Each station appears once; block b holds the stations station_order[b * 16 + j], j < 16. `window_starts`: starts never fall; the first is 0 and the last is 2048; consecutive starts differ by at most 273. Row r is one round of a single round-robin tournament over the 16 blocks: pairing[r, pairing[r, b]] = b, pairing[r, b] != b, and no two rows pair the same two blocks.
All inputs are finite; a program needn't handle non-finite values.
Results may differ from a plain program's by a relative error of at most 0.0049.
Values may be sent and summed in bfloat16 or wider, within the bound.
A program may use at most 128 MiB of HBM per device.

v0:
```python
import math
import jax
import jax.numpy as jnp
from jax import lax
from jax.sharding import PartitionSpec as P

DEC = 4
TAPS = 256
SEG = 2048
BAND = 64
LAGS = 256
ROUNDS = 4
BINS = 1024


def decimate(signal, leading, filter_taps, factor):
    row_count, length = signal.shape
    outputs = length // factor
    per_tile = math.gcd(outputs, 128)
    tile_span = per_tile * factor
    margin = leading.shape[1]
    pieces = 1 + (margin + tile_span - 1) // tile_span
    tile_count = outputs // per_tile
    padded = jnp.concatenate(
        [leading, signal, jnp.zeros((row_count, (pieces - 1) * tile_span - margin), signal.dtype)],
        axis=1,
    )
    tap_count = filter_taps.shape[0]
    positions = jnp.arange(pieces * tile_span, dtype=jnp.int32)[:, None]
    column = jnp.arange(per_tile, dtype=jnp.int32)[None, :]
    tap_index = column * factor + tap_count - 1 - positions
    inside = (tap_index >= 0) & (tap_index < tap_count)
    banded = jnp.where(
        inside,
        jnp.take(filter_taps, jnp.clip(tap_index, 0, tap_count - 1)),
        jnp.zeros((), filter_taps.dtype),
    )
    summed = jnp.zeros((row_count, tile_count, per_tile), jnp.float32)
    for section_index in range(pieces):
        segment = padded[:, section_index * tile_span : section_index * tile_span + length].reshape(
            row_count, tile_count, tile_span
        )
        summed = summed + jnp.einsum(
            "rtu,ui->rti",
            segment,
            banded[section_index * tile_span : (section_index + 1) * tile_span],
            preferred_element_type=jnp.float32,
        )
    return summed.reshape(row_count, outputs)


def dft_matrix(seg_length, bin_count):
    sample = jnp.arange(seg_length, dtype=jnp.int32)
    frequency = jnp.arange(bin_count, dtype=jnp.int32)
    angles = (frequency[:, None] * sample[None, :] % seg_length).astype(jnp.float32) * (
        2.0 * math.pi / seg_length
    )
    taper_curve = 0.5 - 0.5 * jnp.cos(sample.astype(jnp.float32) * (2.0 * math.pi / seg_length))
    joined = jnp.concatenate(
        [jnp.cos(angles) * taper_curve[None, :], -jnp.sin(angles) * taper_curve[None, :]], axis=0
    )
    return joined.astype(jnp.bfloat16)


def lag_matrix(seg_length, bin_count, lag_count, window_count):
    frequency = jnp.arange(bin_count, dtype=jnp.int32)
    lag_offset = jnp.arange(lag_count, dtype=jnp.int32) - lag_count // 2 + seg_length
    angles = (frequency[:, None] * lag_offset[None, :] % seg_length).astype(jnp.float32) * (
        2.0 * math.pi / seg_length
    )
    normalizer = 1.0 / math.sqrt(bin_count * window_count)
    return jnp.stack([jnp.cos(angles) * normalizer, -jnp.sin(angles) * normalizer]).astype(
        jnp.bfloat16
    )


def whiten_flat(spectrum, band_width):
    halves, bin_count, columns = spectrum.shape
    grouped = spectrum.reshape(halves, bin_count // band_width, band_width, columns)
    band_level = jnp.sum(grouped * grouped, axis=(0, 2)) / (2 * band_width)
    scaled = grouped * (1.0 / jnp.sqrt(band_level + 1e-06))[None, :, None]
    return scaled.reshape(spectrum.shape).astype(jnp.bfloat16)


def cross_spectra(left_spec, right_spec):
    turned = jnp.stack([right_spec, jnp.stack([-right_spec[1], right_spec[0]])])
    return jnp.einsum("cfws,kcfwt->kfst", left_spec, turned, preferred_element_type=jnp.float32)


def body(raw_traces, filter_taps, station_order, window_starts, pairing):
    members = lax.axis_size("sta")
    station_count, local_time = raw_traces.shape
    block_size = station_count // members
    margin = TAPS - DEC
    ordered = jnp.take(raw_traces, station_order, axis=0)
    gathered = lax.all_to_all(ordered, "sta", split_axis=0, concat_axis=1, tiled=True)
    leading = jnp.zeros((block_size, margin), gathered.dtype)
    low_rate = decimate(gathered, leading, filter_taps, DEC).astype(jnp.bfloat16)
    window_count = window_starts.shape[0]
    windows = jax.vmap(
        lambda first_sample: lax.dynamic_slice_in_dim(low_rate, first_sample, SEG, 1)
    )(window_starts)
    windows = windows.reshape(window_count * block_size, SEG)
    spectrum = lax.dot_general(
        dft_matrix(SEG, BINS), windows, (((1,), (1,)), ((), ())), preferred_element_type=jnp.float32
    )
    whitened = whiten_flat(spectrum.reshape(2, BINS, window_count * block_size), BAND)
    by_bin = lax.all_to_all(whitened[None], "sta", split_axis=2, concat_axis=0, tiled=True)
    lag_table = lag_matrix(SEG, BINS, LAGS, window_count)
    own_spec = whitened.reshape(2, BINS, window_count, block_size)
    collected = []
    for round_index in range(ROUNDS):
        picked = jnp.take(by_bin, pairing[round_index], axis=0)
        partner_spec = lax.all_to_all(picked, "sta", split_axis=0, concat_axis=2, tiled=True)
        partner_spec = partner_spec.reshape(2, BINS, window_count, block_size)
        cross_spec = cross_spectra(own_spec, partner_spec).astype(jnp.bfloat16)
        collected.append(cross_spec.reshape(2, BINS, block_size * block_size))
    correlated = jnp.einsum(
        "rkfp,kfl->rpl", jnp.stack(collected), lag_table, preferred_element_type=jnp.float32
    )
    return correlated.reshape(ROUNDS, block_size, block_size, LAGS)


def solution(mesh):
    return jax.shard_map(
        body,
        mesh=mesh,
        in_specs=(P("parts", "sta"), P(), P("parts"), P("parts"), P()),
        out_specs=P(None, ("parts", "sta"), None, None),
        check_vma=False,
    )
```

profile of v0, /device:TPU:0, one launch (start us, length us, event | category | flops | bytes accessed | tf_op | source)
XLA Modules:
  0.0 1280.5 jit_solution(12925101330786375420)
XLA Ops:
  3.6 7.4 all-to-all-start
  11.3 35.5 %multiply_convert_fusion.1 = (bf16[1024,2048]{1,0:T(8,128)(2,1)}, bf16[1024,2048]{1,0:T(8,128)(2,1)}) fusion(f32[2048]{0:T(1024)S(1)} %multiply_subtract_fusion), kind=kLoop, calls=%fused_computation.20 | loop fusion | flops 39845888 | bytes 8396800 | tf_op jit(solution)/shard_map/convert.2
  46.8 764.8 %gather_fusion.1 = bf16[131072]{0:T(1024)(128)(2,1)S(1)} fusion(bf16[256]{0:T(256)(128)(2,1)S(1)} %copy-done.2, s32[131072]{0:T(1024)S(1)} %fusion.28), kind=kCustom, calls=%fused_computation.5 | custom fusion | bytes 1048576 | tf_op jit(solution)/shard_map/jit(_take)/gather | solution.py:35
  812.0 8.4 pad_maximum_fusion
  821.7 21.5 %while.1 = (s32[]{:T(128)}, bf16[16,4096]{1,0:T(8,128)(2,1)S(1)}, s32[16,2]{0,1:T(2,128)S(1)}, bf16[16,16,2048]{2,1,0:T(8,128)(2,1)S(1)}, s32[]{:T(128)}) while((s32[]{:T(128)}, bf16[16,4096]{1,0:T(8,128)(2,1)S(1)}, s32[16,2]{0,1:T(2,128)S(1)}, bf16[16,16,2048]{2,1,0:T(8,128)(2,1)S(1)}, s32[]{:T(128)}) %tuple.38), condition=%wide.while_cond, body=%wide.while_body.sunk | while | flops 2 | bytes 131169 | solution.py:101
  857.5 22.9 %all-to-all-done.1 = bf16[1,2,1024,256]{3,1,0,2:T(2,128)(2,1)S(1)} async-done(((bf16[1,2,1024,256]{3,1,0,2:T(2,128)(2,1)}), bf16[1,2,1024,256]{3,1,0,2:T(2,128)(2,1)S(1)}, u32[]{:S(2)}, u32[]{:S(2)}) %all-to-all-start.1) | async-done | bytes 1048608 | tf_op jit(solution)/shard_map/all_to_all | solution.py:108
  897.6 19.0 %all-to-all-done.2 = bf16[16,2,64,256]{3,2,1,0:T(8,128)(2,1)} async-done(((bf16[16,2,64,256]{3,2,1,0:T(8,128)(2,1)}), bf16[16,2,64,256]{3,2,1,0:T(8,128)(2,1)}, u32[]{:S(2)}, u32[]{:S(2)}) %all-to-all-start.2) | async-done | bytes 1048608 | tf_op jit(solution)/shard_map/all_to_all | solution.py:114
  916.6 7.2 all-to-all-start.3
  927.7 19.0 %all-to-all-done.3 = bf16[16,2,64,256]{3,2,1,0:T(8,128)(2,1)} async-done(((bf16[16,2,64,256]{3,2,1,0:T(8,128)(2,1)}), bf16[16,2,64,256]{3,2,1,0:T(8,128)(2,1)}, u32[]{:S(2)}, u32[]{:S(2)}) %all-to-all-start.3) | async-done | bytes 1048608 | tf_op jit(solution)/shard_map/all_to_all | solution.py:114
  946.8 6.9 all-to-all-start.4
  957.6 19.0 %all-to-all-done.4 = bf16[16,2,64,256]{3,2,1,0:T(8,128)(2,1)} async-done(((bf16[16,2,64,256]{3,2,1,0:T(8,128)(2,1)}), bf16[16,2,64,256]{3,2,1,0:T(8,128)(2,1)}, u32[]{:S(2)}, u32[]{:S(2)}) %all-to-all-start.4) | async-done | bytes 1048608 | tf_op jit(solution)/shard_map/all_to_all | solution.py:114
  995.1 12.1 copy.132
  1036.3 32.0 %copy.110 = bf16[2,2,1024,16,16]{3,4,1,0,2:T(8,128)(2,1)} copy(bf16[2,2,1024,16,16]{2,4,3,1,0:T(8,128)(2,1)S(1)} %pad_maximum_fusion.1) | data formatting | bytes 4194304 | tf_op jit(solution)/shard_map/stack | solution.py:86
  1068.3 13.4 %fusion.6 = bf16[2,1024,16,16]{2,3,0,1:T(8,128)(2,1)} fusion(bf16[2,2,1024,16,16]{3,4,1,0,2:T(8,128)(2,1)} %copy.110, bf16[2,1024,16,16,1]{3,2,0,4,1:T(8,128)(2,1)} %copy.132), kind=kOutput, calls=%fused_computation.24 | convolution fusion | flops 34078720 | bytes 4194304 | tf_op jit(solution)/shard_map/cfws,kcfwt->kfst/dot_general | solution.py:87
  1081.7 10.1 copy.112
  1107.8 23.2 %copy.116 = bf16[2,2,1024,16,16]{3,4,1,0,2:T(8,128)(2,1)} copy(bf16[2,2,1024,16,16]{2,4,3,1,0:T(8,128)(2,1)S(1)} %pad_maximum_fusion.2) | data formatting | bytes 4194304 | tf_op jit(solution)/shard_map/stack | solution.py:86
  1131.1 13.4 %fusion.7 = bf16[2,1024,16,16]{2,3,0,1:T(8,128)(2,1)} fusion(bf16[2,2,1024,16,16]{3,4,1,0,2:T(8,128)(2,1)} %copy.116, bf16[2,1024,16,16,1]{3,2,0,4,1:T(8,128)(2,1)} %copy.132), kind=kOutput, calls=%fused_computation.25 | convolution fusion | flops 34078720 | bytes 4194304 | tf_op jit(solution)/shard_map/cfws,kcfwt->kfst/dot_general | solution.py:87
  1144.5 10.3 copy.118
  1170.8 23.2 %copy.122 = bf16[2,2,1024,16,16]{3,4,1,0,2:T(8,128)(2,1)} copy(bf16[2,2,1024,16,16]{2,4,3,1,0:T(8,128)(2,1)S(1)} %pad_maximum_fusion.3) | data formatting | bytes 4194304 | tf_op jit(solution)/shard_map/stack | solution.py:86
  1194.0 13.4 %fusion.8 = bf16[2,1024,16,16]{2,3,0,1:T(8,128)(2,1)} fusion(bf16[2,2,1024,16,16]{3,4,1,0,2:T(8,128)(2,1)} %copy.122, bf16[2,1024,16,16,1]{3,2,0,4,1:T(8,128)(2,1)} %copy.132), kind=kOutput, calls=%fused_computation.26 | convolution fusion | flops 34078720 | bytes 4194304 | tf_op jit(solution)/shard_map/cfws,kcfwt->kfst/dot_general | solution.py:87
  1207.4 10.2 copy.124
  1229.2 23.2 %copy.128 = bf16[2,2,1024,16,16]{3,4,1,0,2:T(8,128)(2,1)} copy(bf16[2,2,1024,16,16]{2,4,3,1,0:T(8,128)(2,1)S(1)} %pad_maximum_fusion.4) | data formatting | bytes 4194304 | tf_op jit(solution)/shard_map/stack | solution.py:86
  1252.5 13.4 %fusion.9 = bf16[2,1024,16,16]{2,3,0,1:T(8,128)(2,1)} fusion(bf16[2,2,1024,16,16]{3,4,1,0,2:T(8,128)(2,1)} %copy.128, bf16[2,1024,16,16,1]{3,2,0,4,1:T(8,128)(2,1)} %copy.132), kind=kOutput, calls=%fused_computation.27 | convolution fusion | flops 34078720 | bytes 4194304 | tf_op jit(solution)/shard_map/cfws,kcfwt->kfst/dot_general | solution.py:87
  1265.9 10.1 copy.130
  (156 shorter events, 161.0 us)
Async XLA Ops:
  0.0 1.5 copy-start
  0.0 46.8 %copy-start.11 = (s32[16]{0:T(128)S(1)}, s32[16]{0:T(128)}, u32[]{:S(2)}) copy-start(s32[16]{0:T(128)} %param.10) | copy-start | bytes 196
  0.0 46.8 %copy-start.2 = (bf16[256]{0:T(256)(128)(2,1)S(1)}, bf16[256]{0:T(256)(128)(2,1)}, u32[]{:S(2)}) copy-start(bf16[256]{0:T(256)(128)(2,1)} %param.8) | copy-start | bytes 1540
  3.6 816.7 %all-to-all-start = ((bf16[16,16,1024]{2,1,0:T(8,128)(2,1)}), bf16[16,16,1024]{2,1,0:T(8,128)(2,1)S(1)}, u32[]{:S(2)}, u32[]{:S(2)}) async-start(bf16[16,16,1024]{2,1,0:T(8,128)(2,1)} %broadcast_select_fusion.4), calls=%async_computation | async-start | bytes 1048576 | tf_op jit(solution)/shard_map/all_to_all | solution.py:96
  843.3 14.2 %copy-start.10 = (s32[4,16]{1,0:T(4,128)S(1)}, s32[4,16]{1,0:T(4,128)}, u32[]{:S(2)}) copy-start(s32[4,16]{1,0:T(4,128)} %param.11) | copy-start | bytes 772
  851.4 29.0 %all-to-all-start.1 = ((bf16[1,2,1024,256]{3,1,0,2:T(2,128)(2,1)}), bf16[1,2,1024,256]{3,1,0,2:T(2,128)(2,1)S(1)}, u32[]{:S(2)}, u32[]{:S(2)}) async-start(bf16[1,2,1024,256]{3,1,0,2:T(2,128)(2,1)} %copy.103), calls=%async_computation.1 | async-start | bytes 2097152 | tf_op jit(solution)/shard_map/all_to_all | solution.py:108
  880.4 1.0 copy-start.6
  886.7 29.9 %all-to-all-start.2 = ((bf16[16,2,64,256]{3,2,1,0:T(8,128)(2,1)}), bf16[16,2,64,256]{3,2,1,0:T(8,128)(2,1)}, u32[]{:S(2)}, u32[]{:S(2)}) async-start(bf16[16,2,64,256]{3,2,1,0:T(8,128)(2,1)} %broadcast_select_fusion.3), calls=%async_computation.2 | async-start | bytes 2097152 | tf_op jit(solution)/shard_map/all_to_all | solution.py:114
  916.6 30.2 %all-to-all-start.3 = ((bf16[16,2,64,256]{3,2,1,0:T(8,128)(2,1)}), bf16[16,2,64,256]{3,2,1,0:T(8,128)(2,1)}, u32[]{:S(2)}, u32[]{:S(2)}) async-start(bf16[16,2,64,256]{3,2,1,0:T(8,128)(2,1)} %broadcast_select_fusion.2), calls=%async_computation.3 | async-start | bytes 2097152 | tf_op jit(solution)/shard_map/all_to_all | solution.py:114
  946.8 29.9 %all-to-all-start.4 = ((bf16[16,2,64,256]{3,2,1,0:T(8,128)(2,1)}), bf16[16,2,64,256]{3,2,1,0:T(8,128)(2,1)}, u32[]{:S(2)}, u32[]{:S(2)}) async-start(bf16[16,2,64,256]{3,2,1,0:T(8,128)(2,1)} %broadcast_select_fusion.1), calls=%async_computation.4 | async-start | bytes 2097152 | tf_op jit(solution)/shard_map/all_to_all | solution.py:114
  976.7 47.8 %all-to-all-start.5 = ((bf16[16,2,64,256]{3,2,1,0:T(8,128)(2,1)}), bf16[16,2,64,256]{3,2,1,0:T(8,128)(2,1)S(1)}, u32[]{:S(2)}, u32[]{:S(2)}) async-start(bf16[16,2,64,256]{3,2,1,0:T(8,128)(2,1)} %broadcast_select_fusion), calls=%async_computation.5 | async-start | bytes 2097152 | tf_op jit(solution)/shard_map/all_to_all | solution.py:114
  1081.7 21.1 %copy-start.5 = (bf16[1,2,16,64,256]{3,2,4,1,0:T(8,128)(2,1)S(1)}, bf16[1,2,16,64,256]{3,2,4,1,0:T(8,128)(2,1)}, u32[]{:S(2)}) copy-start(bf16[1,2,16,64,256]{3,2,4,1,0:T(8,128)(2,1)} %copy.113) | copy-start | bytes 3145732
  1144.5 21.3 %copy-start.4 = (bf16[1,2,16,64,256]{3,2,4,1,0:T(8,128)(2,1)S(1)}, bf16[1,2,16,64,256]{3,2,4,1,0:T(8,128)(2,1)}, u32[]{:S(2)}) copy-start(bf16[1,2,16,64,256]{3,2,4,1,0:T(8,128)(2,1)} %copy.119) | copy-start | bytes 3145732
  1207.4 17.8 %copy-start.3 = (bf16[1,2,16,64,256]{3,2,4,1,0:T(8,128)(2,1)S(1)}, bf16[1,2,16,64,256]{3,2,4,1,0:T(8,128)(2,1)}, u32[]{:S(2)}) copy-start(bf16[1,2,16,64,256]{3,2,4,1,0:T(8,128)(2,1)} %copy.125) | copy-start | bytes 3145732
  1265.9 10.1 copy-start.7
  1265.9 10.1 copy-start.8
  1265.9 10.1 copy-start.9
  1276.0 4.0 copy-start.1
where the time goes:
time: 1290 us; the launch traced here: 1280 us
  local copies, waits for them, and re-layouts  1020 us (79%)
  waiting for transfers between devices  80 us (6%)
  other arithmetic  76.3 us (6%)
  matrix products  64.1 us (5%)
  starting transfers between devices  41.3 us (3%)
    gather x1, local copies, waits for them, and re-layouts, decimate(): jnp.take(filter_taps, jnp.clip(tap_index, 0, tap_count - 1))  765 us
    another operation x8, local copies, waits for them, and re-layouts, cross_spectra(): turned = jnp.stack([right_spec, jnp.stack([-right_spec[1], right_spec[0]])])  113 us
    all_to_all x4, waiting for transfers between devices, body(): lax.all_to_all(picked, 'sta', split_axis=0, concat_axis=2, tiled=True)  57.1 us
    dot_general x4, matrix products, cross_spectra(): jnp.einsum('cfws,kcfwt->kfst', left_spec, turned, preferred_element_type=...  53.7 us
    another operation x2, other arithmetic  41 us
    convert_element_type x4, local copies, waits for them, and re-layouts, body(): cross_spec = cross_spectra(own_spec, partner_spec).astype(jnp.bfloat16)  40.7 us
    all_to_all x4, starting transfers between devices, body(): lax.all_to_all(picked, 'sta', split_axis=0, concat_axis=2, tiled=True)  27.9 us
  transfers between devices with their start and end apart: 6, of which 4 were waited for; matrix products, arithmetic and copies ran while one was open for 67% of the time, Pallas kernels for 0%

commit v1 on v0

--- a/solution.py
+++ b/solution.py
@@ -11,6 +11,29 @@
 LAGS = 256
 ROUNDS = 4
 BINS = 1024
+
+
+def split_up(array, dim, length):
+    shape = array.shape
+    blocks = array.reshape(*shape[:dim], length, shape[dim] // length, *shape[dim + 1 :])
+    return jnp.moveaxis(blocks, dim, 0)
+
+
+def laid_out(blocks, dim):
+    shape = list(blocks.shape[1:])
+    shape[dim] *= blocks.shape[0]
+    return jnp.moveaxis(blocks, 0, dim).reshape(shape)
+
+
+def swapped_with_each(array, axis, split_dim, concat_dim):
+    size, index = (lax.axis_size(axis), lax.axis_index(axis))
+    parts = split_up(array, split_dim, size)
+    outs = [parts[index]]
+    for step in range(1, size):
+        sent = parts[index ^ step]
+        outs.append(lax.ppermute(sent, axis, [(i, i ^ step) for i in range(size)]))
+    parts = jnp.stack(outs)[index ^ jnp.arange(size)]
+    return laid_out(parts, concat_dim)
 
 
 def decimate(signal, leading, filter_taps, factor):
@@ -111,7 +134,7 @@
     collected = []
     for round_index in range(ROUNDS):
         picked = jnp.take(by_bin, pairing[round_index], axis=0)
-        partner_spec = lax.all_to_all(picked, "sta", split_axis=0, concat_axis=2, tiled=True)
+        partner_spec = swapped_with_each(picked, "sta", 0, 2)
         partner_spec = partner_spec.reshape(2, BINS, window_count, block_size)
         cross_spec = cross_spectra(own_spec, partner_spec).astype(jnp.bfloat16)
         collected.append(cross_spec.reshape(2, BINS, block_size * block_size))

time: 1290 us -> 1300 us (level)
  waiting for transfers between devices: 80 us -> 0.16 us
  starting transfers between devices: 41.3 us -> 100 us
  local copies, waits for them, and re-layouts: 1020 us -> 1060 us
    ppermute x0 -> x60, starting transfers between devices: none -> 86.4 us  [swapped_with_each(): outs.append(lax.ppermute(sent, axis, [(i, i ^ step) for i in range(size)]))]
    all_to_all x4 -> x0, waiting for transfers between devices: 57.1 us -> none  [body(): lax.all_to_all(picked, 'sta', split_axis=0, concat_axis=2, tiled=True)]
    unnamed x27 -> x97, local copies, waits for them, and re-layouts: 1.38 us -> 50 us
    all_to_all x4 -> x0, starting transfers between devices: 27.9 us -> none  [body(): lax.all_to_all(picked, 'sta', split_axis=0, concat_axis=2, tiled=True)]
    all_to_all x1, waiting for transfers between devices: 22.9 us -> 0.01 us  [body(): lax.all_to_all(whitened[None], 'sta', split_axis=2, concat_axis=0, tiled=...]
    all_to_all x4 -> x0, local copies, waits for them, and re-layouts: 14.3 us -> none  [body(): lax.all_to_all(picked, 'sta', split_axis=0, concat_axis=2, tiled=True)]
    gather x48 -> x52, local copies, waits for them, and re-layouts: 21.2 us -> 29.5 us
  transfers between devices with their start and end apart: 6 -> 62, of which waited for: 4 -> 0; matrix products, arithmetic and copies ran while one was open for 67% -> 70% of each run, Pallas kernels for 0% -> 0%
where the time goes in v1:
time: 1300 us; the launch traced here: 1290 us
  local copies, waits for them, and re-layouts  1060 us (82%)
  starting transfers between devices  100 us (8%)
  other arithmetic  65 us (5%)
  matrix products  63.8 us (5%)
    gather x1, local copies, waits for them, and re-layouts, decimate(): jnp.take(filter_taps, jnp.clip(tap_index, 0, tap_count - 1))  765 us
    another operation x8, local copies, waits for them, and re-layouts, cross_spectra(): turned = jnp.stack([right_spec, jnp.stack([-right_spec[1], right_spec[0]])])  104 us
    ppermute x60, starting transfers between devices, swapped_with_each(): outs.append(lax.ppermute(sent, axis, [(i, i ^ step) for i in range(size)]))  86.4 us
    dot_general x4, matrix products, cross_spectra(): jnp.einsum('cfws,kcfwt->kfst', left_spec, turned, preferred_element_type=...  53.5 us
    unnamed x97, local copies, waits for them, and re-layouts  50 us
    another operation x2, other arithmetic  41 us
    convert_element_type x4, local copies, waits for them, and re-layouts, body(): cross_spec = cross_spectra(own_spec, partner_spec).astype(jnp.bfloat16)  40.6 us
  transfers between devices with their start and end apart: 62, of which 0 were waited for; matrix products, arithmetic and copies ran while one was open for 70% of the time, Pallas kernels for 0%

profile of v1, /device:TPU:0, one launch (start us, length us, event | category | flops | bytes accessed | tf_op | source)
XLA Modules:
  0.0 1289.8 jit_solution(13758428329623981596)
XLA Ops:
  3.6 7.4 all-to-all-start
  11.3 35.5 %multiply_convert_fusion.1 = (bf16[1024,2048]{1,0:T(8,128)(2,1)}, bf16[1024,2048]{1,0:T(8,128)(2,1)}) fusion(f32[2048]{0:T(1024)S(1)} %multiply_subtract_fusion), kind=kLoop, calls=%fused_computation.24 | loop fusion | flops 39845888 | bytes 8396800 | tf_op jit(solution)/shard_map/convert.2
  46.9 764.8 %gather_fusion.1 = bf16[131072]{0:T(1024)(128)(2,1)S(1)} fusion(bf16[256]{0:T(256)(128)(2,1)S(1)} %copy-done.2, s32[131072]{0:T(1024)S(1)} %fusion.28), kind=kCustom, calls=%fused_computation.5 | custom fusion | bytes 1048576 | tf_op jit(solution)/shard_map/jit(_take)/gather | solution.py:58
  812.0 8.5 pad_maximum_fusion
  821.8 21.5 %while.1 = (s32[]{:T(128)}, bf16[16,4096]{1,0:T(8,128)(2,1)S(1)}, s32[16,2]{0,1:T(2,128)S(1)}, bf16[16,16,2048]{2,1,0:T(8,128)(2,1)S(1)}, s32[]{:T(128)}) while((s32[]{:T(128)}, bf16[16,4096]{1,0:T(8,128)(2,1)S(1)}, s32[16,2]{0,1:T(2,128)S(1)}, bf16[16,16,2048]{2,1,0:T(8,128)(2,1)S(1)}, s32[]{:T(128)}) %tuple.96), condition=%wide.while_cond, body=%wide.while_body.sunk | while | flops 2 | bytes 131169 | solution.py:124
  843.3 5.8 multiply_reduce_fusion
  851.5 6.2 all-to-all-start.1
  857.9 5.5 multiply_convert_fusion.4
  869.5 12.1 copy.263
  1044.3 3.8 copy.250
  1057.9 4.1 stack_reshape_reshape.12
  1063.5 23.3 %copy.241 = bf16[2,2,1024,16,16]{3,4,1,0,2:T(8,128)(2,1)} copy(bf16[2,2,1024,16,16]{2,4,3,1,0:T(8,128)(2,1)S(1)} %pad_maximum_fusion.1) | data formatting | bytes 4194304 | tf_op jit(solution)/shard_map/stack | solution.py:109
  1086.8 13.4 %fusion.6 = bf16[2,1024,16,16]{2,3,0,1:T(8,128)(2,1)} fusion(bf16[2,2,1024,16,16]{3,4,1,0,2:T(8,128)(2,1)} %copy.241, bf16[2,1024,16,16,1]{3,2,0,4,1:T(8,128)(2,1)} %copy.263), kind=kOutput, calls=%fused_computation.28 | convolution fusion | flops 34078720 | bytes 4194304 | tf_op jit(solution)/shard_map/cfws,kcfwt->kfst/dot_general | solution.py:110
  1100.2 10.3 copy.243
  1121.9 23.3 %copy.247 = bf16[2,2,1024,16,16]{3,4,1,0,2:T(8,128)(2,1)} copy(bf16[2,2,1024,16,16]{2,4,3,1,0:T(8,128)(2,1)S(1)} %pad_maximum_fusion.2) | data formatting | bytes 4194304 | tf_op jit(solution)/shard_map/stack | solution.py:109
  1145.2 13.4 %fusion.7 = bf16[2,1024,16,16]{2,3,0,1:T(8,128)(2,1)} fusion(bf16[2,2,1024,16,16]{3,4,1,0,2:T(8,128)(2,1)} %copy.247, bf16[2,1024,16,16,1]{3,2,0,4,1:T(8,128)(2,1)} %copy.263), kind=kOutput, calls=%fused_computation.29 | convolution fusion | flops 34078720 | bytes 4194304 | tf_op jit(solution)/shard_map/cfws,kcfwt->kfst/dot_general | solution.py:110
  1158.6 10.1 copy.249
  1180.4 23.3 %copy.253 = bf16[2,2,1024,16,16]{3,4,1,0,2:T(8,128)(2,1)} copy(bf16[2,2,1024,16,16]{2,4,3,1,0:T(8,128)(2,1)S(1)} %pad_maximum_fusion.3) | data formatting | bytes 4194304 | tf_op jit(solution)/shard_map/stack | solution.py:109
  1203.7 13.4 %fusion.8 = bf16[2,1024,16,16]{2,3,0,1:T(8,128)(2,1)} fusion(bf16[2,2,1024,16,16]{3,4,1,0,2:T(8,128)(2,1)} %copy.253, bf16[2,1024,16,16,1]{3,2,0,4,1:T(8,128)(2,1)} %copy.263), kind=kOutput, calls=%fused_computation.30 | convolution fusion | flops 34078720 | bytes 4194304 | tf_op jit(solution)/shard_map/cfws,kcfwt->kfst/dot_general | solution.py:110
  1217.0 10.1 copy.255
  1238.6 23.3 %copy.259 = bf16[2,2,1024,16,16]{3,4,1,0,2:T(8,128)(2,1)} copy(bf16[2,2,1024,16,16]{2,4,3,1,0:T(8,128)(2,1)S(1)} %pad_maximum_fusion.4) | data formatting | bytes 4194304 | tf_op jit(solution)/shard_map/stack | solution.py:109
  1261.9 13.4 %fusion.9 = bf16[2,1024,16,16]{2,3,0,1:T(8,128)(2,1)} fusion(bf16[2,2,1024,16,16]{3,4,1,0,2:T(8,128)(2,1)} %copy.259, bf16[2,1024,16,16,1]{3,2,0,4,1:T(8,128)(2,1)} %copy.263), kind=kOutput, calls=%fused_computation.31 | convolution fusion | flops 34078720 | bytes 4194304 | tf_op jit(solution)/shard_map/cfws,kcfwt->kfst/dot_general | solution.py:110
  1275.3 10.1 copy.261
  1285.4 4.0 fusion.10
  (350 shorter events, 243.4 us)
Async XLA Ops:
  3.6 816.8 %all-to-all-start = ((bf16[16,16,1024]{2,1,0:T(8,128)(2,1)}), bf16[16,16,1024]{2,1,0:T(8,128)(2,1)S(1)}, u32[]{:S(2)}, u32[]{:S(2)}) async-start(bf16[16,16,1024]{2,1,0:T(8,128)(2,1)} %broadcast_select_fusion.4), calls=%async_computation | async-start | bytes 1048576 | tf_op jit(solution)/shard_map/all_to_all | solution.py:119
  851.5 30.0 %all-to-all-start.1 = ((bf16[1,2,1024,256]{3,1,0,2:T(2,128)(2,1)}), bf16[1,2,1024,256]{3,1,0,2:T(2,128)(2,1)S(1)}, u32[]{:S(2)}, u32[]{:S(2)}) async-start(bf16[1,2,1024,256]{3,1,0,2:T(2,128)(2,1)} %copy.234), calls=%async_computation.1 | async-start | bytes 2097152 | tf_op jit(solution)/shard_map/all_to_all | solution.py:131
  892.6 15.0 %collective-permute-start.3 = (bf16[1,2,64,256]{3,2,1,0:T(8,128)(2,1)S(1)}, bf16[1,2,64,256]{3,2,1,0:T(8,128)(2,1)}, u32[]{:S(2)}, u32[]{:S(2)}) collective-permute-start(bf16[1,2,64,256]{3,2,1,0:T(8,128)(2,1)S(1)} %get-tuple-element.43), channel_id=1, source_target_pairs={{0,4},{1,5},{2,6},{3,7},{4,0},{5,1},{6,2},{7,3},{8,12},{9,13},{10,... | collective-permute-start | bytes 196616 | tf_op jit(solution)/shard_map/ppermute | solution.py:34
  895.0 14.0 %collective-permute-start.4 = (bf16[1,2,64,256]{3,2,1,0:T(8,128)(2,1)S(1)}, bf16[1,2,64,256]{3,2,1,0:T(8,128)(2,1)S(1)}, u32[]{:S(2)}, u32[]{:S(2)}) collective-permute-start(bf16[1,2,64,256]{3,2,1,0:T(8,128)(2,1)S(1)} %get-tuple-element.42), channel_id=1, source_target_pairs={{0,5},{1,4},{2,7},{3,6},{4,1},{5,0},{6,3},{7,2},{8,13},{9,12},{10,... | collective-permute-start | bytes 196616 | tf_op jit(solution)/shard_map/ppermute | solution.py:34
  897.6 14.4 %collective-permute-start.5 = (bf16[1,2,64,256]{3,2,1,0:T(8,128)(2,1)S(1)}, bf16[1,2,64,256]{3,2,1,0:T(8,128)(2,1)S(1)}, u32[]{:S(2)}, u32[]{:S(2)}) collective-permute-start(bf16[1,2,64,256]{3,2,1,0:T(8,128)(2,1)S(1)} %get-tuple-element.41), channel_id=1, source_target_pairs={{0,6},{1,7},{2,4},{3,5},{4,2},{5,3},{6,0},{7,1},{8,14},{9,15},{10,... | collective-permute-start | bytes 196616 | tf_op jit(solution)/shard_map/ppermute | solution.py:34
  903.2 13.6 %collective-permute-start.7 = (bf16[1,2,64,256]{3,2,1,0:T(8,128)(2,1)S(1)}, bf16[1,2,64,256]{3,2,1,0:T(8,128)(2,1)S(1)}, u32[]{:S(2)}, u32[]{:S(2)}) collective-permute-start(bf16[1,2,64,256]{3,2,1,0:T(8,128)(2,1)S(1)} %get-tuple-element.39), channel_id=1, source_target_pairs={{0,8},{1,9},{2,10},{3,11},{4,12},{5,13},{6,14},{7,15},{8,0},{9,1},... | collective-permute-start | bytes 196616 | tf_op jit(solution)/shard_map/ppermute | solution.py:34
  909.0 13.5 %collective-permute-start.9 = (bf16[1,2,64,256]{3,2,1,0:T(8,128)(2,1)S(1)}, bf16[1,2,64,256]{3,2,1,0:T(8,128)(2,1)S(1)}, u32[]{:S(2)}, u32[]{:S(2)}) collective-permute-start(bf16[1,2,64,256]{3,2,1,0:T(8,128)(2,1)S(1)} %get-tuple-element.37), channel_id=1, source_target_pairs={{0,10},{1,11},{2,8},{3,9},{4,14},{5,15},{6,12},{7,13},{8,2},{9,3},... | collective-permute-start | bytes 196616 | tf_op jit(solution)/shard_map/ppermute | solution.py:34
  960.1 14.6 %collective-permute-start.32 = (bf16[1,2,64,256]{3,2,1,0:T(8,128)(2,1)}, bf16[1,2,64,256]{3,2,1,0:T(8,128)(2,1)}, u32[]{:S(2)}, u32[]{:S(2)}) collective-permute-start(bf16[1,2,64,256]{3,2,1,0:T(8,128)(2,1)} %get-tuple-element.78), channel_id=1, source_target_pairs={{0,3},{1,2},{2,1},{3,0},{4,7},{5,6},{6,5},{7,4},{8,11},{9,10},{10,... | collective-permute-start | bytes 196616 | tf_op jit(solution)/shard_map/ppermute | solution.py:34
  960.7 17.6 %collective-permute-start.33 = (bf16[1,2,64,256]{3,2,1,0:T(8,128)(2,1)}, bf16[1,2,64,256]{3,2,1,0:T(8,128)(2,1)}, u32[]{:S(2)}, u32[]{:S(2)}) collective-permute-start(bf16[1,2,64,256]{3,2,1,0:T(8,128)(2,1)} %get-tuple-element.77), channel_id=1, source_target_pairs={{0,4},{1,5},{2,6},{3,7},{4,0},{5,1},{6,2},{7,3},{8,12},{9,13},{10,... | collective-permute-start | bytes 196616 | tf_op jit(solution)/shard_map/ppermute | solution.py:34
  965.1 15.1 %collective-permute-start.34 = (bf16[1,2,64,256]{3,2,1,0:T(8,128)(2,1)}, bf16[1,2,64,256]{3,2,1,0:T(8,128)(2,1)}, u32[]{:S(2)}, u32[]{:S(2)}) collective-permute-start(bf16[1,2,64,256]{3,2,1,0:T(8,128)(2,1)} %get-tuple-element.76), channel_id=1, source_target_pairs={{0,5},{1,4},{2,7},{3,6},{4,1},{5,0},{6,3},{7,2},{8,13},{9,12},{10,... | collective-permute-start | bytes 196616 | tf_op jit(solution)/shard_map/ppermute | solution.py:34
  969.0 13.8 %collective-permute-start.35 = (bf16[1,2,64,256]{3,2,1,0:T(8,128)(2,1)}, bf16[1,2,64,256]{3,2,1,0:T(8,128)(2,1)S(1)}, u32[]{:S(2)}, u32[]{:S(2)}) collective-permute-start(bf16[1,2,64,256]{3,2,1,0:T(8,128)(2,1)} %get-tuple-element.75), channel_id=1, source_target_pairs={{0,6},{1,7},{2,4},{3,5},{4,2},{5,3},{6,0},{7,1},{8,14},{9,15},{10,... | collective-permute-start | bytes 196616 | tf_op jit(solution)/shard_map/ppermute | solution.py:34
  971.3 14.6 %collective-permute-start.36 = (bf16[1,2,64,256]{3,2,1,0:T(8,128)(2,1)}, bf16[1,2,64,256]{3,2,1,0:T(8,128)(2,1)S(1)}, u32[]{:S(2)}, u32[]{:S(2)}) collective-permute-start(bf16[1,2,64,256]{3,2,1,0:T(8,128)(2,1)} %get-tuple-element.74), channel_id=1, source_target_pairs={{0,7},{1,6},{2,5},{3,4},{4,3},{5,2},{6,1},{7,0},{8,15},{9,14},{10,... | collective-permute-start | bytes 196616 | tf_op jit(solution)/shard_map/ppermute | solution.py:34
  974.7 13.6 %collective-permute-start.37 = (bf16[1,2,64,256]{3,2,1,0:T(8,128)(2,1)}, bf16[1,2,64,256]{3,2,1,0:T(8,128)(2,1)S(1)}, u32[]{:S(2)}, u32[]{:S(2)}) collective-permute-start(bf16[1,2,64,256]{3,2,1,0:T(8,128)(2,1)} %get-tuple-element.73), channel_id=1, source_target_pairs={{0,8},{1,9},{2,10},{3,11},{4,12},{5,13},{6,14},{7,15},{8,0},{9,1},... | collective-permute-start | bytes 196616 | tf_op jit(solution)/shard_map/ppermute | solution.py:34
  980.2 13.4 %collective-permute-start.39 = (bf16[1,2,64,256]{3,2,1,0:T(8,128)(2,1)}, bf16[1,2,64,256]{3,2,1,0:T(8,128)(2,1)S(1)}, u32[]{:S(2)}, u32[]{:S(2)}) collective-permute-start(bf16[1,2,64,256]{3,2,1,0:T(8,128)(2,1)} %get-tuple-element.71), channel_id=1, source_target_pairs={{0,10},{1,11},{2,8},{3,9},{4,14},{5,15},{6,12},{7,13},{8,2},{9,3},... | collective-permute-start | bytes 196616 | tf_op jit(solution)/shard_map/ppermute | solution.py:34
  982.9 13.6 %collective-permute-start.40 = (bf16[1,2,64,256]{3,2,1,0:T(8,128)(2,1)}, bf16[1,2,64,256]{3,2,1,0:T(8,128)(2,1)S(1)}, u32[]{:S(2)}, u32[]{:S(2)}) collective-permute-start(bf16[1,2,64,256]{3,2,1,0:T(8,128)(2,1)} %get-tuple-element.70), channel_id=1, source_target_pairs={{0,11},{1,10},{2,9},{3,8},{4,15},{5,14},{6,13},{7,12},{8,3},{9,2},... | collective-permute-start | bytes 196616 | tf_op jit(solution)/shard_map/ppermute | solution.py:34
  998.5 15.4 %collective-permute-start.47 = (bf16[1,2,64,256]{3,2,1,0:T(8,128)(2,1)}, bf16[1,2,64,256]{3,2,1,0:T(8,128)(2,1)}, u32[]{:S(2)}, u32[]{:S(2)}) collective-permute-start(bf16[1,2,64,256]{3,2,1,0:T(8,128)(2,1)} %get-tuple-element.95), channel_id=1, source_target_pairs={{0,3},{1,2},{2,1},{3,0},{4,7},{5,6},{6,5},{7,4},{8,11},{9,10},{10,... | collective-permute-start | bytes 196616 | tf_op jit(solution)/shard_map/ppermute | solution.py:34
  1000.2 17.1 %collective-permute-start.48 = (bf16[1,2,64,256]{3,2,1,0:T(8,128)(2,1)}, bf16[1,2,64,256]{3,2,1,0:T(8,128)(2,1)}, u32[]{:S(2)}, u32[]{:S(2)}) collective-permute-start(bf16[1,2,64,256]{3,2,1,0:T(8,128)(2,1)} %get-tuple-element.94), channel_id=1, source_target_pairs={{0,4},{1,5},{2,6},{3,7},{4,0},{5,1},{6,2},{7,3},{8,12},{9,13},{10,... | collective-permute-start | bytes 196616 | tf_op jit(solution)/shard_map/ppermute | solution.py:34
  1002.8 16.9 %collective-permute-start.49 = (bf16[1,2,64,256]{3,2,1,0:T(8,128)(2,1)}, bf16[1,2,64,256]{3,2,1,0:T(8,128)(2,1)}, u32[]{:S(2)}, u32[]{:S(2)}) collective-permute-start(bf16[1,2,64,256]{3,2,1,0:T(8,128)(2,1)} %get-tuple-element.93), channel_id=1, source_target_pairs={{0,5},{1,4},{2,7},{3,6},{4,1},{5,0},{6,3},{7,2},{8,13},{9,12},{10,... | collective-permute-start | bytes 196616 | tf_op jit(solution)/shard_map/ppermute | solution.py:34
  1008.5 13.8 %collective-permute-start.50 = (bf16[1,2,64,256]{3,2,1,0:T(8,128)(2,1)}, bf16[1,2,64,256]{3,2,1,0:T(8,128)(2,1)S(1)}, u32[]{:S(2)}, u32[]{:S(2)}) collective-permute-start(bf16[1,2,64,256]{3,2,1,0:T(8,128)(2,1)} %get-tuple-element.92), channel_id=1, source_target_pairs={{0,6},{1,7},{2,4},{3,5},{4,2},{5,3},{6,0},{7,1},{8,14},{9,15},{10,... | collective-permute-start | bytes 196616 | tf_op jit(solution)/shard_map/ppermute | solution.py:34
  1010.6 14.6 %collective-permute-start.51 = (bf16[1,2,64,256]{3,2,1,0:T(8,128)(2,1)}, bf16[1,2,64,256]{3,2,1,0:T(8,128)(2,1)S(1)}, u32[]{:S(2)}, u32[]{:S(2)}) collective-permute-start(bf16[1,2,64,256]{3,2,1,0:T(8,128)(2,1)} %get-tuple-element.91), channel_id=1, source_target_pairs={{0,7},{1,6},{2,5},{3,4},{4,3},{5,2},{6,1},{7,0},{8,15},{9,14},{10,... | collective-permute-start | bytes 196616 | tf_op jit(solution)/shard_map/ppermute | solution.py:34
  1013.9 13.8 %collective-permute-start.52 = (bf16[1,2,64,256]{3,2,1,0:T(8,128)(2,1)}, bf16[1,2,64,256]{3,2,1,0:T(8,128)(2,1)S(1)}, u32[]{:S(2)}, u32[]{:S(2)}) collective-permute-start(bf16[1,2,64,256]{3,2,1,0:T(8,128)(2,1)} %get-tuple-element.90), channel_id=1, source_target_pairs={{0,8},{1,9},{2,10},{3,11},{4,12},{5,13},{6,14},{7,15},{8,0},{9,1},... | collective-permute-start | bytes 196616 | tf_op jit(solution)/shard_map/ppermute | solution.py:34
  1019.7 13.7 %collective-permute-start.54 = (bf16[1,2,64,256]{3,2,1,0:T(8,128)(2,1)S(1)}, bf16[1,2,64,256]{3,2,1,0:T(8,128)(2,1)S(1)}, u32[]{:S(2)}, u32[]{:S(2)}) collective-permute-start(bf16[1,2,64,256]{3,2,1,0:T(8,128)(2,1)S(1)} %get-tuple-element.88), channel_id=1, source_target_pairs={{0,10},{1,11},{2,8},{3,9},{4,14},{5,15},{6,12},{7,13},{8,2},{9,3},... | collective-permute-start | bytes 196616 | tf_op jit(solution)/shard_map/ppermute | solution.py:34
  1022.3 13.4 %collective-permute-start.55 = (bf16[1,2,64,256]{3,2,1,0:T(8,128)(2,1)S(1)}, bf16[1,2,64,256]{3,2,1,0:T(8,128)(2,1)S(1)}, u32[]{:S(2)}, u32[]{:S(2)}) collective-permute-start(bf16[1,2,64,256]{3,2,1,0:T(8,128)(2,1)S(1)} %get-tuple-element.87), channel_id=1, source_target_pairs={{0,11},{1,10},{2,9},{3,8},{4,15},{5,14},{6,13},{7,12},{8,3},{9,2},... | collective-permute-start | bytes 196616 | tf_op jit(solution)/shard_map/ppermute | solution.py:34
  1033.5 14.7 %collective-permute-start.59 = (bf16[1,2,64,256]{3,2,1,0:T(8,128)(2,1)S(1)}, bf16[1,2,64,256]{3,2,1,0:T(8,128)(2,1)S(1)}, u32[]{:S(2)}, u32[]{:S(2)}) collective-permute-start(bf16[1,2,64,256]{3,2,1,0:T(8,128)(2,1)S(1)} %get-tuple-element.83), channel_id=1, source_target_pairs={{0,15},{1,14},{2,13},{3,12},{4,11},{5,10},{6,9},{7,8},{8,7},{9,6},... | collective-permute-start | bytes 196616 | tf_op jit(solution)/shard_map/ppermute | solution.py:34
  (55 other events, 683.1 us)
